TPU v7x, 32 devices: a whole 2x2x4 slice. The times are simulated.
32 devices in a mesh: box: 8 (over z, y), dir: 4 (over x, core).
Axes of the slice: x: 2, y: 2, z: 4, core: 2. Of those that a mesh axis runs over, the one named last changes fastest.
Arguments:
- coarse_field: float32 [512, 2, 4, 2048], P('box', None, None, 'dir'), may hold values from -6 to 6
- trans_table: float32 [316, 2, 2048], P(None, None, 'dir'), may hold values from -1.5 to 1.5
- partner_ids: int32 [512, 30], P('box'), may hold values from 0 to 511, as said below
- partner_types: int32 [512, 30], P('box'), may hold values from 0 to 315
- partner_count: int32 [512], P('box'), may hold values from 15 to 30
- child_count: int32 [512], P('box'), may hold values from 1 to 7, as said below
- child_octant: int32 [2048], P('box'), may hold values from 0 to 7
- dir_angles: float32 [2, 2048], replicated, may hold values from -3.140625 to 3.140625
- stencil_ids: int32 [2048, 4], replicated, may hold values from 0 to 511, as said below
- stencil_weights: float32 [2048, 4], replicated, may hold values from -1.8 to 1.8
Outputs:
- fine_field: float32 [2048, 2, 4, 512], P(('box', 'dir'))
Inputs may be any that keep to these rules, and one draw needn't show every extreme that they name: `partner_ids`: coarse box b sits on a grid whose z coordinate takes the two highest bits of b (the higher one as its bit 1) and whose x and y coordinates take the lower bits in turn (x from bit 0, y from bit 1, x from bit 2, and so on); the slots of b name distinct boxes that are children of neighbours of b's parent and not adjacent to b. `child_count`: each aligned block of 64 coarse boxes has exactly 256 children in all. stencil_ids[c, s] lies within 2 of c // 4, counted circularly over 512 directions.
All inputs are finite; a program needn't handle non-finite values.
Results may differ from a plain program's by a relative error of at most 0.0003.
Values sent between devices are 32-bit elements; how exact they have to be, the bound alone decides.
No kernel may reach another device: no remote copies, remote signals or barrier semaphores. Data moves between devices by JAX's collectives and lax.ppermute only.
A program may use at most 64 MiB of HBM per device.

v0:
```python
import jax
import jax.numpy as jnp
from jax import lax
from jax.sharding import PartitionSpec as P

wave_scale = 3.0


def padded(block, sides, width):
    for axis, dim in sides:
        count = lax.axis_size(axis)
        forward = [(i, i + 1) for i in range(count - 1)]
        forward.append((count - 1, 0))
        backward = [(target, source) for source, target in forward]
        low = lax.ppermute(
            lax.slice_in_dim(block, block.shape[dim] - width, None, axis=dim), axis, forward
        )
        high = lax.ppermute(lax.slice_in_dim(block, 0, width, axis=dim), axis, backward)
        block = jnp.concatenate([low, block, high], axis=dim)
    return block


def interp_matrix(stencil_ids, stencil_weights, targets):
    matrix = jnp.zeros((stencil_ids.shape[0], targets.shape[0]), jnp.float32)
    for point in range(stencil_ids.shape[1]):
        matrix = matrix + jnp.where(
            stencil_ids[:, point, None] == targets[None, :], stencil_weights[:, point, None], 0.0
        )
    return matrix


def shift_children(coarse_rows, parent_local, child_octant, theta_cols, phi_cols):
    sign_x = 1.0 - 2.0 * (child_octant % 2).astype(jnp.float32)
    sign_y = 1.0 - 2.0 * (child_octant // 2 % 2).astype(jnp.float32)
    sign_z = 1.0 - 2.0 * (child_octant // 4).astype(jnp.float32)
    unit_x = jnp.sin(theta_cols) * jnp.cos(phi_cols)
    unit_y = jnp.sin(theta_cols) * jnp.sin(phi_cols)
    unit_z = jnp.cos(theta_cols)
    phase_angle = wave_scale * (
        sign_x[:, None] * unit_x[None, :]
        + sign_y[:, None] * unit_y[None, :]
        + sign_z[:, None] * unit_z[None, :]
    )
    cosine = jnp.cos(phase_angle)[:, None, :]
    sine = jnp.sin(phase_angle)[:, None, :]
    coarse_count = coarse_rows.shape[0]
    select = (parent_local[:, None] == jnp.arange(coarse_count, dtype=jnp.int32)[None, :]).astype(
        jnp.float32
    )
    flat_rows = coarse_rows.reshape(coarse_count, -1)
    gathered = jnp.dot(
        select, flat_rows, precision=lax.Precision.HIGHEST, preferred_element_type=jnp.float32
    )
    gathered = gathered.reshape((parent_local.shape[0],) + coarse_rows.shape[1:])
    real_part = gathered[:, 0] * cosine + gathered[:, 1] * sine
    imag_part = gathered[:, 1] * cosine - gathered[:, 0] * sine
    return jnp.stack([real_part, imag_part], axis=1)


def per_device(
    coarse_field,
    trans_table,
    partner_ids,
    partner_types,
    partner_count,
    child_count,
    child_octant,
    dir_angles,
    stencil_ids,
    stencil_weights,
):
    box_rows = coarse_field.shape[0]
    source_count = coarse_field.shape[2]
    kc_dev = coarse_field.shape[3]
    full_kc = stencil_ids.shape[0]
    fine_count = full_kc // 4
    type_count = trans_table.shape[0]
    dir_index = lax.axis_index("dir")
    sources = lax.all_gather(coarse_field, "box", axis=0, tiled=True)
    live_mask = (
        jnp.arange(partner_ids.shape[1], dtype=jnp.int32)[None, :] < partner_count[:, None]
    ).astype(jnp.float32)
    flat_sources = sources.reshape(sources.shape[0], -1)
    flat_table = trans_table.reshape(type_count, -1)
    type_range = jnp.arange(type_count, dtype=jnp.int32)

    def translate(running, column):
        part_ids, type_ids, weight = column
        source = jnp.take(flat_sources, part_ids, axis=0).reshape(
            (box_rows, 2, source_count, kc_dev)
        )
        type_pick = (type_ids[:, None] == type_range[None, :]).astype(jnp.float32) * weight[:, None]
        tab_row = jnp.dot(
            type_pick,
            flat_table,
            precision=lax.Precision.HIGHEST,
            preferred_element_type=jnp.float32,
        ).reshape((box_rows, 2, kc_dev))
        table_real = tab_row[:, 0, None, :]
        table_imag = tab_row[:, 1, None, :]
        real_part = table_real * source[:, 0] + table_imag * source[:, 1]
        imag_part = table_real * source[:, 1] - table_imag * source[:, 0]
        return (running + jnp.stack([real_part, imag_part], axis=1), None)

    zeros_init = jnp.zeros(coarse_field.shape, jnp.float32)
    translated, _ = lax.scan(translate, zeros_init, (partner_ids.T, partner_types.T, live_mask.T))
    fine_rows = child_octant.shape[0]
    bounds = jnp.cumsum(child_count)
    parent_local = jnp.sum(
        (bounds[None, :] <= jnp.arange(fine_rows, dtype=jnp.int32)[:, None]).astype(jnp.int32),
        axis=1,
    )
    rim_width = 8
    widened = padded(translated, (("dir", 3),), rim_width)
    columns = (
        dir_index * kc_dev - rim_width + jnp.arange(kc_dev + 2 * rim_width, dtype=jnp.int32)
    ) % full_kc
    shifted = shift_children(
        widened,
        parent_local,
        child_octant,
        jnp.take(dir_angles[0], columns),
        jnp.take(dir_angles[1], columns),
    )
    kf_dev = fine_count // lax.axis_size("dir")
    targets = dir_index * kf_dev + jnp.arange(kf_dev, dtype=jnp.int32)
    matrix = interp_matrix(
        jnp.take(stencil_ids, columns, axis=0), jnp.take(stencil_weights, columns, axis=0), targets
    )
    local_fine = jnp.einsum("rtnc,cf->rtnf", shifted, matrix, precision=lax.Precision.HIGHEST)
    fine_field = lax.all_to_all(local_fine, "dir", split_axis=0, concat_axis=3, tiled=True)
    return fine_field


def solution(mesh):
    placed = (
        P("box", None, None, "dir"),
        P(None, None, "dir"),
        P("box", None),
        P("box", None),
        P("box"),
        P("box"),
        P("box"),
        P(),
        P(),
        P(),
    )
    return jax.shard_map(
        per_device,
        mesh=mesh,
        in_specs=placed,
        out_specs=P(("box", "dir"), None, None, None),
        check_vma=False,
    )
```

profile of v0, /device:TPU:11, one launch (start us, length us, event | category | flops | bytes accessed | tf_op | source)
XLA Modules:
  0.0 586.3 jit_solution(13856329016170378469)
XLA Ops:
  27.8 105.5 %all-gather.2.cloned.1.call-done = f32[512,2,4,512]{3,2,1,0:T(4,128)} async-done(((f32[64,2,4,512]{3,2,1,0:T(4,128)}), f32[512,2,4,512]{3,2,1,0:T(4,128)}) %all-gather.2.cloned.1.call-update) | async-done | bytes 8388624 | tf_op jit(solution)/shard_map/all_gather | solution.py:79
  133.3 10.9 %reshape.279 = f32[512,4096]{1,0:T(8,128)} reshape(f32[512,2,4,512]{3,2,1,0:T(4,128)} %all-gather.2.cloned.1.call-done) | data formatting | bytes 16777216 | tf_op jit(solution)/shard_map/reshape | solution.py:83
  144.2 391.3 %while.11 = (s32[]{:T(128)}, f32[64,2,4,512]{3,2,1,0:T(4,128)}, s32[30,64]{1,0:T(8,128)}, f32[30,64]{1,0:T(8,128)S(1)}, f32[316,1024]{1,0:T(8,128)S(1)}, /*index...) while((s32[]{:T(128)}, f32[64,2,4,512]{3,2,1,0:T(4,128)}, s32[30,64]{1,0:T(8,128)}, ...), condition=%wide.region_3.4_spmd.clone, body=%wide.region_2.3_spmd.clone.sunk | while | flops 250389568 | bytes 23845972 | solution.py:106
  148.9 4.8 gather_fusion
  162.0 4.8 gather_fusion
  175.0 4.8 gather_fusion
  188.1 4.8 gather_fusion
  201.1 4.8 gather_fusion
  214.2 4.8 gather_fusion
  227.2 4.8 gather_fusion
  240.2 4.8 gather_fusion
  253.3 4.8 gather_fusion
  266.3 4.8 gather_fusion
  279.4 4.8 gather_fusion
  292.4 4.8 gather_fusion
  305.5 4.8 gather_fusion
  318.5 4.8 gather_fusion
  331.5 4.8 gather_fusion
  344.6 4.8 gather_fusion
  357.6 4.8 gather_fusion
  370.7 4.8 gather_fusion
  383.7 4.8 gather_fusion
  552.5 9.6 %fusion.11 = f32[256,2,4,128]{3,0,2,1:T(8,128)S(1)} fusion(f32[256,1,4,528]{0,3,2,1:T(8,128)S(1)} %get-tuple-element.104, f32[256,1,4,528]{0,3,2,1:T(8,128)S(1)} %get-tuple-element.103, f32[528]{0:T(1024)S(1)} %copy-done.14, f32[528]{0:T(1024)S(1)} %copy-done.15, f32[528]{0:T(1024)S(1)} %copy-done.16, f32[528]{0:T(1024)S(1)} %copy-done.13, ...), kind=kOutput, calls=%fused_computation.29 | convolution fusion | flops 1662769152 | bytes 5391360 | tf_op jit(solution)/shard_map/rtnc,cf->rtnf/dot_general | solution.py:130
  562.8 15.4 %all_to_all.18 = f32[256,2,4,128]{3,2,1,0:T(4,128)S(1)} all-to-all(f32[256,2,4,128]{3,2,1,0:T(4,128)S(1)} %copy.30), channel_id=1, replica_groups=mesh['box'=8,'dir'=4] {'dir'}, dimensions={0} | all-to-all | bytes 2097152 | tf_op jit(solution)/shard_map/all_to_all | solution.py:131
  (659 shorter events, 337.8 us)
Async XLA Ops:
  6.5 126.8 %all-gather.2.cloned.1.call-start = ((), (), s32[]{:S(2)}) async-start(), calls=%async_computation.1 | async-start | bytes 9437184 | tf_op jit(solution)/shard_map/all_gather | solution.py:79
  11.7 3.6 copy-start.19
  11.7 3.9 copy-start.7
  11.7 4.3 copy-start.8
  16.4 3.8 copy-start.5
  20.2 1.5 copy-start.6
  21.0 3.5 copy-start.18
  21.0 3.5 copy-start.20
  154.4 1.3 copy-start
  167.5 1.3 copy-start
  180.5 1.3 copy-start
  193.6 1.3 copy-start
  206.6 1.3 copy-start
  219.7 1.3 copy-start
  232.7 1.3 copy-start
  245.7 1.3 copy-start
  258.8 1.3 copy-start
  271.8 1.3 copy-start
  284.9 1.3 copy-start
  536.8 5.5 collective-permute-start
  538.0 7.8 %collective-permute-start.1 = (f32[64,2,4,8]{3,2,1,0:T(4,128)S(1)}, f32[64,2,4,8]{3,2,1,0:T(4,128)S(1)}, u32[]{:S(2)}, u32[]{:S(2)}) collective-permute-start(f32[64,2,4,8]{3,2,1,0:T(4,128)S(1)} %get-tuple-element.106), channel_id=1, source_target_pairs={{1,0},{2,1},{3,2},{0,3},{5,4},{6,5},{7,6},{4,7},{9,8},{10,9},{11,1... | collective-permute-start | bytes 49160 | tf_op jit(solution)/shard_map/ppermute | solution.py:18
  547.9 1.8 copy-start.17
  549.7 2.1 copy-start.3
  549.7 2.1 copy-start.4
  (87 other events, 91.2 us)
Sparse Core Ops, SparseCore 0:
  9.5 123.8 all-gather.1
where the time goes:
time: 596 us; the launch traced here: 586 us
  local copies, waits for them, and re-layouts  279 us (47%)
  other arithmetic  119 us (20%)
  waiting for transfers between devices  114 us (19%)
  matrix products  41.6 us (7%)
  blocking collectives  15.4 us (3%)
  between operations  13.8 us (2%)
    gather x60, local copies, waits for them, and re-layouts, translate(): jnp.take(flat_sources, part_ids, axis=0)  164 us
    all_gather x1, waiting for transfers between devices, per_device(): sources = lax.all_gather(coarse_field, 'box', axis=0, tiled=True)  106 us
    select_n x60, other arithmetic, translate(): jnp.take(flat_sources, part_ids, axis=0)  51 us
    while x210, local copies, waits for them, and re-layouts  49.2 us
    and x30, other arithmetic, translate(): jnp.take(flat_sources, part_ids, axis=0)  36.9 us
    dot_general x30, matrix products, translate(): jnp.dot(type_pick, flat_table, precision=lax.Precision.HIGHEST, preferred...  30 us
    eq x30, local copies, waits for them, and re-layouts, translate(): type_ids[:, None] == type_range[None, :]  20.7 us
    all_to_all x1, blocking collectives, per_device(): lax.all_to_all(local_fine, 'dir', split_axis=0, concat_axis=3, tiled=True)  15.4 us
  transfers between devices with their start and end apart: 3, of which 3 were waited for; matrix products, arithmetic and copies ran while one was open for 3% of the time, Pallas kernels for 0%

commit v1 on v0

v1 whole, which is shorter than its diff:
```python
import functools

import jax
import jax.numpy as jnp
from jax import lax
from jax.experimental import pallas as pl
from jax.experimental.pallas import tpu as pltpu
from jax.sharding import Mesh
from jax.sharding import PartitionSpec as P

wave_scale = 3.0
planes = 4
lanes = 128
half = 4
rim = 2


def up(size, step):
    return -(-size // step) * step


def edge_bits(rows):
    bits = rows.bit_length() - 1
    return bits, [place for place in range(2, bits) if place % 2 == bits % 2]


def near_edge(block, ring):
    bits, fixed = edge_bits(block.shape[0])
    tail = block.shape[1:]
    picked = block.reshape((2,) * bits + tail)
    for place in fixed:
        picked = lax.dynamic_index_in_dim(picked, 1 - ring, axis=bits - 1 - place, keepdims=True)
    return picked.reshape((block.shape[0] >> len(fixed),) + tail)


def edge_rank(local, rows):
    bits, fixed = edge_bits(rows)
    rank = jnp.zeros_like(local)
    taken = 0
    for place in range(bits):
        if place not in fixed:
            rank = rank + (local // 2**place % 2) * 2**taken
            taken += 1
    return rank


def split(value):
    high = value.astype(jnp.bfloat16)
    low = (value - high.astype(jnp.float32)).astype(jnp.bfloat16)
    return high, low


def three_pass(left, right, dims):
    dot = functools.partial(
        lax.dot_general, dimension_numbers=(dims, ((), ())), preferred_element_type=jnp.float32
    )
    return dot(left[0], right[0]) + (dot(left[0], right[1]) + dot(left[1], right[0]))


def fine_kernel(
    rows, slots, fine_rows, piece_count, first, meta, *refs
):
    pieces = refs[:piece_count]
    tab_re, tab_im, cosine, sine, matrix, spill_re, spill_im, out = refs[piece_count : piece_count + 8]
    field, sems, moved, swapped, shifted = refs[piece_count + 8 :]
    copies = []
    start = 0
    for index, piece in enumerate(pieces):
        size = piece.shape[0]
        copies.append(pltpu.make_async_copy(piece, field.at[pl.ds(start, size)], sems.at[index]))
        copies[-1].start()
        start += size
    for copy in copies:
        copy.wait()

    sub = lax.broadcasted_iota(jnp.int32, (2 * half, lanes), 0)
    sign = jnp.where(sub < half, 1.0, -1.0).astype(jnp.float32)
    pairs = rows * slots
    stride = 2 * pairs + rows + 2 * fine_rows
    fixed_slots = slots // 2
    group = 5 if (slots - fixed_slots) % 5 == 0 else 1
    weights = split(matrix[...])
    spill_re_parts = split(spill_re[...])
    spill_im_parts = split(spill_im[...])
    dest_count = out.shape[1]
    dest_rows = fine_rows // dest_count

    def plane_step(plane, unused):
        base = plane * stride

        def box_step(box, unused):
            place = base + box * slots

            def add(slot, sums):
                row = meta[place + slot]
                kind = meta[place + pairs + slot]
                value = field[row]
                return sums[0] + tab_re[kind] * value, sums[1] + tab_im[kind] * value

            sums = (jnp.zeros((2 * half, lanes), jnp.float32),) * 2
            for slot in range(fixed_slots):
                sums = add(slot, sums)

            def more(turn, sums):
                for slot in range(group):
                    sums = add(fixed_slots + turn * group + slot, sums)
                return sums

            sums = lax.fori_loop(0, meta[base + 2 * pairs + box], more, sums)
            total = sums[0] + sign * pltpu.roll(sums[1], half, 0)
            moved[box] = total
            swapped[box] = pltpu.roll(total, half, 0)
            return unused

        lax.fori_loop(0, rows, box_step, 0)

        def fine_step(fine, unused):
            place = base + 2 * pairs + rows + fine
            parent = meta[place]
            octant = meta[place + fine_rows]
            shifted[pl.ds(pl.multiple_of(fine * 2 * half, 2 * half), 2 * half), :] = (
                moved[parent] * cosine[octant] + swapped[parent] * sine[octant]
            )
            return unused

        lax.fori_loop(0, fine_rows, fine_step, 0, unroll=8)
        spill = jnp.zeros((2 * half, fine_rows), jnp.float32)
        for part in range(2):
            left = jnp.concatenate(
                [
                    shifted[pl.ds(part * half + block, fine_rows, stride=2 * half), :]
                    for block in range(half)
                ],
                axis=1,
            )
            left = split(left)
            result = three_pass(left, weights, ((1,), (0,)))
            spill = spill + three_pass((spill_re_parts, spill_im_parts)[part], left, ((1,), (1,)))
            for dest in range(dest_count):
                out[plane, dest, part * dest_rows : (part + 1) * dest_rows, :] = result[
                    dest * dest_rows : (dest + 1) * dest_rows
                ]
        for dest in range(dest_count):
            out[plane, dest, 2 * dest_rows :, :] = jnp.concatenate(
                [
                    spill[:, dest * dest_rows : (dest + 1) * dest_rows],
                    jnp.zeros((2 * half, out.shape[3] - dest_rows), jnp.float32),
                ],
                axis=1,
            )
        return unused

    lax.fori_loop(0, planes, plane_step, 0)


def per_device(
    coarse_field,
    trans_table,
    partner_ids,
    partner_types,
    partner_count,
    child_count,
    child_octant,
    dir_angles,
    stencil_ids,
    stencil_weights,
):
    rows, _, source_count, kc_dev = coarse_field.shape
    slots = partner_ids.shape[1]
    type_count = trans_table.shape[0]
    fine_rows = child_octant.shape[0]
    ring_count = lax.axis_size("ring")
    dir_count = lax.axis_size("dir")
    zed = lax.axis_index("zed")
    ring = lax.axis_index("ring")
    dir_index = lax.axis_index("dir")
    fine_count = stencil_ids.shape[0] // 4
    kf_dev = fine_count // dir_count
    kc_pad = up(kc_dev, half * lanes)
    kf_pad = up(kf_dev, lanes)
    pad_dirs = kc_pad - kc_dev
    assert source_count == planes and kc_pad == half * lanes
    dest_rows = fine_rows // dir_count

    def to_blocks(piece):
        piece = jnp.pad(piece, ((0, 0), (0, 0), (0, pad_dirs)))
        return piece.reshape(rows, 2 * half, lanes)

    sent = [
        to_blocks(lax.dynamic_index_in_dim(coarse_field, zed ^ step, axis=2, keepdims=False))
        for step in range(planes)
    ]
    if ring_count == 2:
        sent_edges = [near_edge(piece, ring) for piece in sent]

    def hop(piece, step, ring_step):
        if step == 0 and ring_step == 0:
            return piece
        pairs = [
            (z * ring_count + r, (z ^ step) * ring_count + (r ^ ring_step))
            for z in range(planes)
            for r in range(ring_count)
        ]
        return lax.ppermute(piece, ("zed", "ring"), pairs)

    plane_of = partner_ids // (ring_count * rows)
    ring_of = partner_ids // rows % ring_count
    local = partner_ids % rows
    live = jnp.arange(slots, dtype=jnp.int32)[None, :] < partner_count[:, None]
    if ring_count == 2:
        edge_rows = rows >> len(edge_bits(rows)[1])
        place = jnp.where(
            ring_of == ring,
            plane_of * rows + local,
            planes * rows + plane_of * edge_rows + edge_rank(local, rows),
        )
    else:
        place = partner_ids
    place = jnp.where(live, place, 0)
    kinds = jnp.where(live, partner_types, type_count)
    fixed_slots = slots // 2
    group = 5 if (slots - fixed_slots) % 5 == 0 else 1
    turns = jnp.maximum((partner_count - fixed_slots + group - 1) // group, 0)
    order = jnp.arange(rows, dtype=jnp.int32)
    bounds = jnp.sum(jnp.where(order[None, :] <= order[:, None], child_count[None, :], 0), axis=1)
    parent = jnp.sum(
        (bounds[None, :] <= jnp.arange(fine_rows, dtype=jnp.int32)[:, None]).astype(jnp.int32), axis=1
    )
    meta = jnp.concatenate([place.reshape(-1), kinds.reshape(-1), turns, parent, child_octant])
    meta = lax.all_gather(meta, "zed", axis=0, tiled=True)

    arrived = [hop(piece, step, 0) for step, piece in enumerate(sent)]
    natural = [None] * planes
    stacked = jnp.stack(arrived)
    natural = [lax.dynamic_index_in_dim(stacked, zed ^ plane, axis=0, keepdims=False) for plane in range(planes)]
    if ring_count == 2:
        edges = jnp.stack([hop(piece, step, 1) for step, piece in enumerate(sent_edges)])
        natural += [
            lax.dynamic_index_in_dim(edges, zed ^ plane, axis=0, keepdims=False) for plane in range(planes)
        ]
    else:
        natural = [lax.all_gather(piece, "ring", axis=0, tiled=True) for piece in natural]

    def doubled(table, sign):
        table = jnp.pad(table, ((0, 0), (0, pad_dirs))).reshape(-1, half, lanes)
        return jnp.concatenate([table, sign * table], axis=1)

    padded_table = jnp.pad(trans_table, ((0, 1), (0, 0), (0, 0)))
    tab_re = doubled(padded_table[:, 0], 1.0)
    tab_im = doubled(padded_table[:, 1], 1.0)
    angles = lax.dynamic_slice_in_dim(dir_angles, dir_index * kc_dev, kc_dev, axis=1)
    octants = jnp.arange(8, dtype=jnp.int32)
    sign_x = 1.0 - 2.0 * (octants % 2).astype(jnp.float32)
    sign_y = 1.0 - 2.0 * (octants // 2 % 2).astype(jnp.float32)
    sign_z = 1.0 - 2.0 * (octants // 4).astype(jnp.float32)
    unit_x = jnp.sin(angles[0]) * jnp.cos(angles[1])
    unit_y = jnp.sin(angles[0]) * jnp.sin(angles[1])
    unit_z = jnp.cos(angles[0])
    phase = wave_scale * (
        sign_x[:, None] * unit_x[None, :] + sign_y[:, None] * unit_y[None, :] + sign_z[:, None] * unit_z[None, :]
    )
    cosine = doubled(jnp.cos(phase), 1.0)
    sine = doubled(jnp.sin(phase), -1.0)

    ids = lax.dynamic_slice_in_dim(stencil_ids, dir_index * kc_dev, kc_dev, axis=0).T
    weights = lax.dynamic_slice_in_dim(stencil_weights, dir_index * kc_dev, kc_dev, axis=0).T

    def interp(targets):
        matrix = jnp.zeros((targets.shape[0], kc_dev), jnp.float32)
        for point in range(ids.shape[0]):
            matrix = matrix + jnp.where(
                ids[point][None, :] == targets[:, None], weights[point][None, :], 0.0
            )
        return jnp.pad(matrix, ((0, 0), (0, pad_dirs)))

    first_fine = dir_index * kf_dev
    own = jnp.arange(kf_dev, dtype=jnp.int32)
    outside = jnp.concatenate(
        [jnp.arange(-rim, 0, dtype=jnp.int32), jnp.arange(kf_dev, kf_dev + rim, dtype=jnp.int32)]
    )
    matrix = jnp.pad(interp(first_fine + own).T, ((0, 0), (0, kf_pad - kf_dev)))
    spill = interp((first_fine + outside) % fine_count)
    blank = jnp.zeros_like(spill)
    spill_re = jnp.concatenate([spill, blank], axis=0)
    spill_im = jnp.concatenate([blank, spill], axis=0)

    field_rows = sum(piece.shape[0] for piece in natural)
    whole = pl.BlockSpec(memory_space=pltpu.VMEM)
    local_fine = pl.pallas_call(
        functools.partial(fine_kernel, rows, slots, fine_rows, len(natural), 0),
        out_shape=jax.ShapeDtypeStruct((planes, dir_count, 2 * dest_rows + 2 * half, kf_pad), jnp.float32),
        in_specs=[pl.BlockSpec(memory_space=pltpu.SMEM)]
        + [pl.BlockSpec(memory_space=pl.ANY)] * len(natural)
        + [whole] * 7,
        out_specs=whole,
        scratch_shapes=[
            pltpu.VMEM((field_rows, 2 * half, lanes), jnp.float32),
            pltpu.SemaphoreType.DMA((len(natural),)),
            pltpu.VMEM((rows, 2 * half, lanes), jnp.float32),
            pltpu.VMEM((rows, 2 * half, lanes), jnp.float32),
            pltpu.VMEM((fine_rows * 2 * half, lanes), jnp.float32),
        ],
        compiler_params=pltpu.CompilerParams(vmem_limit_bytes=48 * 2**20),
        name="translate_and_interpolate",
    )(meta, *natural, tab_re, tab_im, cosine, sine, matrix, spill_re, spill_im)

    local_fine = local_fine.reshape((planes * dir_count,) + local_fine.shape[2:])
    parts = lax.all_to_all(local_fine, ("zed", "dir"), split_axis=0, concat_axis=0, tiled=True)
    parts = parts.reshape((planes, dir_count) + parts.shape[1:])
    main = parts[:, :, : 2 * dest_rows, :kf_dev].reshape(planes, dir_count, 2, dest_rows, kf_dev)
    over = parts[:, :, 2 * dest_rows :, :dest_rows].reshape(planes, dir_count, 2, 2 * rim, dest_rows)
    low = jnp.roll(over[:, :, :, :rim], -1, axis=1)
    high = jnp.roll(over[:, :, :, rim:], 1, axis=1)
    middle = jnp.zeros((planes, dir_count, 2, kf_dev - 2 * rim, dest_rows), jnp.float32)
    fix = jnp.concatenate([high, middle, low], axis=3)
    total = main.transpose(3, 2, 0, 1, 4) + fix.transpose(4, 2, 0, 1, 3)
    return total.reshape(dest_rows, 2, source_count, fine_count)


def solution(mesh):
    boxes, dirs = mesh.shape["box"], mesh.shape["dir"]
    fine_mesh = Mesh(mesh.devices.reshape(planes, boxes // planes, dirs), ("zed", "ring", "dir"))
    box = ("zed", "ring")
    placed = (
        P(box, None, None, "dir"),
        P(None, None, "dir"),
        P(box, None),
        P(box, None),
        P(box),
        P(box),
        P(box),
        P(),
        P(),
        P(),
    )
    return jax.shard_map(
        per_device,
        mesh=fine_mesh,
        in_specs=placed,
        out_specs=P(("zed", "ring", "dir"), None, None, None),
        check_vma=False,
    )
```

time: 596 us -> 144 us (0.24); the launches traced: 586 us -> 143 us
  local copies, waits for them, and re-layouts: 279 us -> 27.5 us
  other arithmetic: 119 us -> 11 us
  waiting for transfers between devices: 114 us -> 42.7 us
  matrix products: 41.6 us -> 0 us
  Pallas kernels: 0 us -> 31.6 us
  blocking collectives: 15.4 us -> 0 us
  starting transfers between devices: 1.38 us -> 15.5 us
    gather x64 -> x0, local copies, waits for them, and re-layouts: 175 us -> none  [the longest x60 164 us: translate(): jnp.take(flat_sources, part_ids, axis=0)]
    all_gather x1 -> x0, waiting for transfers between devices: 106 us -> none  [per_device(): sources = lax.all_gather(coarse_field, 'box', axis=0, tiled=True)]
    select_n x64 -> x2, other arithmetic: 51.3 us -> 0.92 us  [the longest x1 0.84 us: per_device(): kinds = jnp.where(live, partner_types, type_count)]
    while x210 -> x0, local copies, waits for them, and re-layouts: 49.2 us -> none
    dot_general x32 -> x0, matrix products: 41.6 us -> none  [the longest x30 30 us: translate(): jnp.dot(type_pick, flat_table, precision=lax.Precision.HIGHEST, preferred...]
    and x31 -> x0, other arithmetic: 36.9 us -> none  [the longest x30 36.9 us: translate(): jnp.take(flat_sources, part_ids, axis=0)]
    pallas_call x0 -> x1, Pallas kernels: none -> 31.6 us  [per_device(): pl.pallas_call(functools.partial(fine_kernel, rows, slots, fine_rows, len...]
    all_to_all x0 -> x1, waiting for transfers between devices: none -> 26.3 us  [per_device(): lax.all_to_all(local_fine, ('zed', 'dir'), split_axis=0, concat_axis=0, t...]
  transfers between devices with their start and end apart: 3 -> 9, of which waited for: 3 -> 4; matrix products, arithmetic and copies ran while one was open for 3% -> 14% of each run, Pallas kernels for 0% -> 0%
where the time goes in v1:
time: 144 us; the launch traced here: 143 us
  waiting for transfers between devices  42.7 us (30%)
  Pallas kernels  31.6 us (22%)
  local copies, waits for them, and re-layouts  27.5 us (19%)
  starting transfers between devices  15.5 us (11%)
  between operations  14.3 us (10%)
  other arithmetic  11 us (8%)
    pallas_call x1, Pallas kernels, per_device(): pl.pallas_call(functools.partial(fine_kernel, rows, slots, fine_rows, len...  31.6 us
    all_to_all x1, waiting for transfers between devices, per_device(): lax.all_to_all(local_fine, ('zed', 'dir'), split_axis=0, concat_axis=0, t...  26.3 us
    ppermute x7, waiting for transfers between devices, hop(): return lax.ppermute(piece, ('zed', 'ring'), pairs)  16.2 us
    unnamed x41, local copies, waits for them, and re-layouts  11.7 us
    all_to_all x1, starting transfers between devices, per_device(): lax.all_to_all(local_fine, ('zed', 'dir'), split_axis=0, concat_axis=0, t...  8.35 us
    ppermute x7, starting transfers between devices, hop(): return lax.ppermute(piece, ('zed', 'ring'), pairs)  7.16 us
    dynamic_slice x1, local copies, waits for them, and re-layouts, per_device(): lax.dynamic_index_in_dim(coarse_field, zed ^ step, axis=2, keepdims=False)  4.98 us
    concatenate x3, other arithmetic, doubled(): return jnp.concatenate([table, sign * table], axis=1)  2.99 us
  transfers between devices with their start and end apart: 9, of which 4 were waited for; matrix products, arithmetic and copies ran while one was open for 14% of the time, Pallas kernels for 0%

profile of v1, /device:TPU:11, one launch (start us, length us, event | category | flops | bytes accessed | tf_op | source)
XLA Modules:
  0.0 142.6 jit_solution(5042320937147504183)
XLA Ops:
  9.4 1.2 dynamic-slice
  13.2 5.0 %constant_dynamic-slice_fusion.7 = (f32[64,2,1,512]{3,2,1,0:T(1,128)S(1)}, f32[64,2,1,512]{3,2,1,0:T(1,128)}, f32[64,2,1,512]{3,2,1,0:T(1,128)}, f32[64,2,1,512]{3,2,1,0:T(1,128)}) fusion(f32[64,2,4,512]{3,2,1,0:T(4,128)} %param.10, s32[]{:T(128)S(6)} %select_n.196, s32[]{:T(128)S(6)} %select_n.197, s32[]{:T(128)S(6)} %select_n.199, s32[]{:T(128)S(6)} %select_n.198), kind=kLoop, calls=%fused_computation.95 | loop fusion | bytes 2097168 | tf_op jit(solution)/shard_map/jit(dynamic_index_in_dim)/dynamic_slice | solution.py:190
  18.2 1.3 collective-permute-start.2
  19.5 1.0 collective-permute-start.1
  20.4 1.1 collective-permute-start
  22.4 2.1 %collective-permute-start.6 = (f32[16,8,128]{2,1,0:T(8,128)S(1)}, f32[16,8,128]{2,1,0:T(8,128)}, u32[]{:S(2)}, u32[]{:S(2)}) collective-permute-start(f32[16,8,128]{2,1,0:T(8,128)S(1)} %bitcast.75), channel_id=1, source_target_pairs={{0,28},{4,24},{8,20},{12,16},{16,12},{20,8},{24,4},{28,0},{1,29},{... | collective-permute-start | bytes 196616 | tf_op jit(solution)/shard_map/ppermute | solution.py:204
  25.4 1.2 collective-permute-start.5
  26.6 0.9 constant_dynamic-slice_fusion.2
  27.5 1.8 %pad_slice_fusion = (f32[317,1,512]{2,1,0:T(1,128)S(1)}, f32[317,1,512]{2,1,0:T(1,128)}) fusion(f32[316,2,512]{2,1,0:T(2,128)S(1)} %copy-done.13), kind=kLoop, calls=%fused_computation.5 | loop fusion | bytes 2592768 | tf_op jit(solution)/shard_map/slice | solution.py:250
  29.4 0.9 cosine_multiply_fusion
  32.5 1.3 select_add_fusion.refs_12_
  34.0 1.8 %pad_maximum_fusion = (f32[317,8,128]{2,1,0:T(8,128)S(1)}, f32[317,8,128]{2,1,0:T(8,128)S(1)}) fusion(f32[317,4,128]{2,1,0:T(4,128)} %bitcast.68, f32[317,4,128]{2,1,0:T(4,128)S(1)} %bitcast.67), kind=kLoop, calls=%fused_computation | loop fusion | flops 649216 | bytes 3895296 | tf_op jit(solution)/shard_map/concatenate | solution.py:246
  36.3 12.9 %collective-permute-done.6 = f32[16,8,128]{2,1,0:T(8,128)} collective-permute-done((f32[16,8,128]{2,1,0:T(8,128)S(1)}, f32[16,8,128]{2,1,0:T(8,128)}, u32[]{:S(2)}, u32[]{:S(2)}) %collective-permute-start.6) | collective-permute-done | bytes 65568 | tf_op jit(solution)/shard_map/ppermute | solution.py:204
  50.3 3.3 %collective-permute-done.4 = f32[16,8,128]{2,1,0:T(8,128)S(1)} collective-permute-done((f32[16,8,128]{2,1,0:T(8,128)S(1)}, f32[16,8,128]{2,1,0:T(8,128)S(1)}, u32[]{:S(2)}, u32[]{:S(2)}) %collective-permute-start.4) | collective-permute-done | bytes 65568 | tf_op jit(solution)/shard_map/ppermute | solution.py:204
  53.6 0.9 pad_maximum_fusion.3
  55.2 1.2 pad_maximum_fusion.2
  57.3 0.9 copy-done.2
  58.3 0.9 copy-done.3
  62.4 0.9 copy-done.8
  64.7 31.6 %translate_and_interpolate.1 = f32[4,4,136,128]{3,2,1,0:T(8,128)S(1)} custom-call(s32[17664]{0:T(1024)S(1)} %copy-done.8, f32[64,8,128]{2,1,0:T(8,128)S(1)} %copy-done.2, f32[64,8,128]{2,1,0:T(8,128)S(1)} %get-tuple-element.9.refs_1_, f32[64,8,128]{2,1,0:T(8,128)S(1)} %get-tuple-element.8.refs_2_, f32[64,8,128]{2,1,0:T(8,128)S(1)} %get-tuple-element.7.refs_3_, ...), custom_call_target="tpu_custom_call" | custom-call | tf_op jit(solution)/shard_map/translate_and_interpolate/pallas_call | solution.py:289
  96.3 1.0 copy-done.1
  97.3 8.3 %all-to-all-start = ((f32[16,136,128]{2,1,0:T(8,128)}), f32[16,136,128]{2,1,0:T(8,128)S(1)}, u32[]{:S(2)}, u32[]{:S(2)}) async-start(f32[16,136,128]{2,1,0:T(8,128)} %bitcast.63), calls=%async_computation | async-start | bytes 2228224 | tf_op jit(solution)/shard_map/all_to_all | solution.py:308
  105.8 26.3 %all-to-all-done = f32[16,136,128]{2,1,0:T(8,128)S(1)} async-done(((f32[16,136,128]{2,1,0:T(8,128)}), f32[16,136,128]{2,1,0:T(8,128)S(1)}, u32[]{:S(2)}, u32[]{:S(2)}) %all-to-all-start) | async-done | bytes 1114144 | tf_op jit(solution)/shard_map/all_to_all | solution.py:308
  134.2 1.6 %reshape.225 = f32[64,2,4,512]{3,2,1,0:T(4,128)} reshape(f32[64,2,4,4,128]{4,3,2,1,0:T(4,128)S(1)} %copy.43) | data formatting | bytes 2097152 | tf_op jit(solution)/shard_map/reshape | solution.py:317
  (82 shorter events, 18.8 us)
Async XLA Ops:
  6.5 25.2 %copy-start = (f32[2048,4]{0,1:T(4,128)S(1)}, f32[2048,4]{0,1:T(4,128)}, u32[]{:S(2)}) copy-start(f32[2048,4]{0,1:T(4,128)} %param.19) | copy-start | bytes 98308
  6.5 50.8 %all-reduce.6.cloned.1.call-start = ((), (), s32[]{:S(2)}) async-start(), calls=%async_computation.1 | async-start | bytes 147456
  13.2 14.3 %copy-start.13 = (f32[316,2,512]{2,1,0:T(2,128)S(1)}, f32[316,2,512]{2,1,0:T(2,128)}, u32[]{:S(2)}) copy-start(f32[316,2,512]{2,1,0:T(2,128)} %param.11) | copy-start | bytes 3883012
  18.2 11.2 %copy-start.11 = (f32[64,2,1,512]{3,2,1,0:T(1,128)}, f32[64,2,1,512]{3,2,1,0:T(1,128)S(1)}, u32[]{:S(2)}) copy-start(f32[64,2,1,512]{3,2,1,0:T(1,128)S(1)} %get-tuple-element.11) | copy-start | bytes 786436
  18.2 37.0 %collective-permute-start.2 = (f32[64,8,128]{2,1,0:T(8,128)}, f32[64,8,128]{2,1,0:T(8,128)}, u32[]{:S(2)}, u32[]{:S(2)}) collective-permute-start(f32[64,8,128]{2,1,0:T(8,128)} %bitcast.6), channel_id=1, source_target_pairs={{0,24},{4,28},{8,16},{12,20},{16,8},{20,12},{24,0},{28,4},{1,25},{... | collective-permute-start | bytes 786440 | tf_op jit(solution)/shard_map/ppermute | solution.py:204
  19.5 35.7 %collective-permute-start.1 = (f32[64,8,128]{2,1,0:T(8,128)}, f32[64,8,128]{2,1,0:T(8,128)}, u32[]{:S(2)}, u32[]{:S(2)}) collective-permute-start(f32[64,8,128]{2,1,0:T(8,128)} %bitcast.4), channel_id=1, source_target_pairs={{0,16},{4,20},{8,24},{12,28},{16,0},{20,4},{24,8},{28,12},{1,17},{... | collective-permute-start | bytes 786440 | tf_op jit(solution)/shard_map/ppermute | solution.py:204
  20.4 34.7 %collective-permute-start = (f32[64,8,128]{2,1,0:T(8,128)}, f32[64,8,128]{2,1,0:T(8,128)}, u32[]{:S(2)}, u32[]{:S(2)}) collective-permute-start(f32[64,8,128]{2,1,0:T(8,128)} %bitcast.2), channel_id=1, source_target_pairs={{0,8},{4,12},{8,0},{12,4},{16,24},{20,28},{24,16},{28,20},{1,9},{5... | collective-permute-start | bytes 786440 | tf_op jit(solution)/shard_map/ppermute | solution.py:204
  22.4 26.8 %collective-permute-start.6 = (f32[16,8,128]{2,1,0:T(8,128)S(1)}, f32[16,8,128]{2,1,0:T(8,128)}, u32[]{:S(2)}, u32[]{:S(2)}) collective-permute-start(f32[16,8,128]{2,1,0:T(8,128)S(1)} %bitcast.75), channel_id=1, source_target_pairs={{0,28},{4,24},{8,20},{12,16},{16,12},{20,8},{24,4},{28,0},{1,29},{... | collective-permute-start | bytes 196616 | tf_op jit(solution)/shard_map/ppermute | solution.py:204
  25.4 23.8 %collective-permute-start.5 = (f32[16,8,128]{2,1,0:T(8,128)S(1)}, f32[16,8,128]{2,1,0:T(8,128)}, u32[]{:S(2)}, u32[]{:S(2)}) collective-permute-start(f32[16,8,128]{2,1,0:T(8,128)S(1)} %bitcast.73), channel_id=1, source_target_pairs={{0,20},{4,16},{8,28},{12,24},{16,4},{20,0},{24,12},{28,8},{1,21},{... | collective-permute-start | bytes 196616 | tf_op jit(solution)/shard_map/ppermute | solution.py:204
  33.9 15.7 %copy-start.15 = (f32[8,4,128]{2,1,0:T(4,128)S(1)}, f32[8,4,128]{2,1,0:T(4,128)}, u32[]{:S(2)}) copy-start(f32[8,4,128]{2,1,0:T(4,128)} %get-tuple-element.36) | copy-start | bytes 49156
  33.9 15.7 %copy-start.16 = (f32[8,4,128]{2,1,0:T(4,128)S(1)}, f32[8,4,128]{2,1,0:T(4,128)}, u32[]{:S(2)}) copy-start(f32[8,4,128]{2,1,0:T(4,128)} %get-tuple-element.37) | copy-start | bytes 49156
  35.7 19.4 %copy-start.12 = (f32[64,2,1,512]{3,2,1,0:T(1,128)S(1)}, f32[64,2,1,512]{3,2,1,0:T(1,128)}, u32[]{:S(2)}) copy-start(f32[64,2,1,512]{3,2,1,0:T(1,128)} %copy-done.11) | copy-start | bytes 786436
  49.3 4.3 %collective-permute-start.4 = (f32[16,8,128]{2,1,0:T(8,128)S(1)}, f32[16,8,128]{2,1,0:T(8,128)S(1)}, u32[]{:S(2)}, u32[]{:S(2)}) collective-permute-start(f32[16,8,128]{2,1,0:T(8,128)S(1)} %bitcast.76), channel_id=1, source_target_pairs={{0,12},{4,8},{8,4},{12,0},{16,28},{20,24},{24,20},{28,16},{1,13},{... | collective-permute-start | bytes 196616 | tf_op jit(solution)/shard_map/ppermute | solution.py:204
  49.3 4.3 %collective-permute-start.3 = (f32[16,8,128]{2,1,0:T(8,128)S(1)}, f32[16,8,128]{2,1,0:T(8,128)S(1)}, u32[]{:S(2)}, u32[]{:S(2)}) collective-permute-start(f32[16,8,128]{2,1,0:T(8,128)S(1)} %bitcast.74), channel_id=1, source_target_pairs={{0,4},{4,0},{8,12},{12,8},{16,20},{20,16},{24,28},{28,24},{1,5},{5... | collective-permute-start | bytes 196616 | tf_op jit(solution)/shard_map/ppermute | solution.py:204
  57.3 0.9 copy-start.2
  58.3 0.9 copy-start.3
  59.2 0.8 copy-start.4
  60.1 0.8 copy-start.5
  60.9 0.8 copy-start.6
  61.7 0.8 copy-start.7
  62.4 0.9 copy-start.8
  63.3 0.7 copy-start.9
  96.3 1.0 copy-start.1
  97.3 34.7 %all-to-all-start = ((f32[16,136,128]{2,1,0:T(8,128)}), f32[16,136,128]{2,1,0:T(8,128)S(1)}, u32[]{:S(2)}, u32[]{:S(2)}) async-start(f32[16,136,128]{2,1,0:T(8,128)} %bitcast.63), calls=%async_computation | async-start | bytes 2228224 | tf_op jit(solution)/shard_map/all_to_all | solution.py:308
  (2 other events, 1.3 us)
Sparse Core Ops, SparseCore 0:
  13.3 43.9 all-reduce.5

commit v2 on v1

v2 whole, which is shorter than its diff:
```python
import functools

import jax
import jax.numpy as jnp
from jax import lax
from jax.experimental import pallas as pl
from jax.experimental.pallas import tpu as pltpu
from jax.sharding import Mesh
from jax.sharding import PartitionSpec as P

wave_scale = 3.0
planes = 4
lanes = 128
half = 4
rim = 2


def up(size, step):
    return -(-size // step) * step


def edge_bits(rows):
    bits = rows.bit_length() - 1
    return bits, [place for place in range(2, bits) if place % 2 == bits % 2]


def near_edge(block, ring):
    count, rows = block.shape[:2]
    bits, fixed = edge_bits(rows)
    tail = block.shape[2:]
    picked = block.reshape((count,) + (2,) * bits + tail)
    for place in fixed:
        picked = lax.dynamic_index_in_dim(picked, 1 - ring, axis=bits - place, keepdims=True)
    return picked.reshape((count, rows >> len(fixed)) + tail)


def edge_rank(local, rows):
    bits, fixed = edge_bits(rows)
    rank = jnp.zeros_like(local)
    taken = 0
    for place in range(bits):
        if place not in fixed:
            rank = rank + (local // 2**place % 2) * 2**taken
            taken += 1
    return rank


def split(value):
    high = value.astype(jnp.bfloat16)
    low = (value - high.astype(jnp.float32)).astype(jnp.bfloat16)
    return high, low


def three_pass(left, right, dims):
    dot = functools.partial(
        lax.dot_general, dimension_numbers=(dims, ((), ())), preferred_element_type=jnp.float32
    )
    return dot(left[0], right[0]) + (dot(left[0], right[1]) + dot(left[1], right[0]))


def pack_kernel(source_count, field, out, whole):
    rows, _, _, width = field.shape
    stride = 2 * source_count

    def row_step(row, unused):
        both = jnp.concatenate([field[row, 0], field[row, 1]], axis=0)
        for block in range(half):
            whole[block, pl.ds(pl.multiple_of(row * stride, stride), stride), :] = both[
                :, block * lanes : (block + 1) * lanes
            ]
        return unused

    lax.fori_loop(0, rows, row_step, 0, unroll=8)
    for source in range(source_count):
        for part in range(2):
            for block in range(half):
                out[source, pl.ds(part * half + block, rows, stride=2 * half), :] = whole[
                    block, pl.ds(part * source_count + source, rows, stride=stride), :
                ]


def fine_kernel(rows, slots, fine_rows, meta_stride, piece_count, meta, *refs):
    pieces = refs[:piece_count]
    table, cosine, sine, matrix, spill_re, spill_im, out = refs[piece_count : piece_count + 7]
    field, turned, sems, moved, swapped, shifted = refs[piece_count + 7 :]
    copies = []
    start = 0
    for index, piece in enumerate(pieces):
        size = piece.shape[0]
        copies.append(pltpu.make_async_copy(piece, field.at[pl.ds(start, size)], sems.at[index]))
        copies[-1].start()
        start += size
    for copy in copies:
        copy.wait()

    def turn_step(row, unused):
        turned[row] = pltpu.roll(field[row], half, 0)
        return unused

    lax.fori_loop(0, start, turn_step, 0, unroll=8)
    sub = lax.broadcasted_iota(jnp.int32, (2 * half, lanes), 0)
    pairs = rows * slots
    weights = split(matrix[...])
    spill_parts = (split(spill_re[...]), split(spill_im[...]))
    dest_count = out.shape[1]
    dest_rows = fine_rows // dest_count

    def plane_step(plane, unused):
        base = plane * meta_stride

        def box_step(box, unused):
            place = base + box * slots
            straight = jnp.zeros((2 * half, lanes), jnp.float32)
            crossed = straight
            for slot in range(slots):
                row = meta[place + slot]
                factor = table[meta[place + pairs + slot]]
                straight = straight + factor * field[row]
                crossed = crossed + factor * turned[row]
            total = jnp.where(
                sub < half,
                straight + pltpu.roll(straight, half, 0),
                pltpu.roll(crossed, half, 0) - crossed,
            )
            moved[box] = total
            swapped[box] = pltpu.roll(total, half, 0)
            return unused

        lax.fori_loop(0, rows, box_step, 0, unroll=2)

        def fine_step(fine, unused):
            place = base + 2 * pairs + fine
            parent = meta[place]
            octant = meta[place + fine_rows]
            shifted[pl.ds(pl.multiple_of(fine * 2 * half, 2 * half), 2 * half), :] = (
                moved[parent] * cosine[octant] + swapped[parent] * sine[octant]
            )
            return unused

        lax.fori_loop(0, fine_rows, fine_step, 0, unroll=8)
        spill = jnp.zeros((2 * half, fine_rows), jnp.float32)
        for part in range(2):
            left = jnp.concatenate(
                [
                    shifted[pl.ds(part * half + block, fine_rows, stride=2 * half), :]
                    for block in range(half)
                ],
                axis=1,
            )
            left = split(left)
            result = three_pass(left, weights, ((1,), (0,)))
            spill = spill + three_pass(spill_parts[part], left, ((1,), (1,)))
            for dest in range(dest_count):
                out[plane, dest, part * dest_rows : (part + 1) * dest_rows, :] = result[
                    dest * dest_rows : (dest + 1) * dest_rows
                ]
        for dest in range(dest_count):
            out[plane, dest, 2 * dest_rows :, :] = jnp.concatenate(
                [
                    spill[:, dest * dest_rows : (dest + 1) * dest_rows],
                    jnp.zeros((2 * half, out.shape[3] - dest_rows), jnp.float32),
                ],
                axis=1,
            )
        return unused

    lax.fori_loop(0, planes, plane_step, 0)


def join_kernel(source_count, parts, out, whole):
    dest_rows = out.shape[0]
    dirs = parts.shape[0] // source_count
    over = jnp.concatenate(
        [parts[index, 2 * dest_rows :, :lanes] for index in range(parts.shape[0])], axis=0
    ).T[:dest_rows]
    lane = lax.broadcasted_iota(jnp.int32, (dest_rows, lanes), 1)
    for source in range(source_count):
        for part in range(2):
            turned = []
            for index in range(dirs):
                first = (source * dirs + index) * 2 * half + part * half
                turned.append(pltpu.roll(over, (lanes - rim - first) % lanes, 1))
            for index in range(dirs):
                fix = jnp.where(lane < rim, turned[index - 1], 0.0) + jnp.where(
                    lane >= lanes - rim, turned[(index + 1) % dirs], 0.0
                )
                whole[
                    index, pl.ds(part * source_count + source, dest_rows, stride=2 * source_count), :
                ] = parts[source * dirs + index, part * dest_rows : (part + 1) * dest_rows, :] + fix

    def row_step(row, unused):
        start = pl.multiple_of(row * 2 * source_count, 2 * source_count)
        both = jnp.concatenate(
            [whole[index, pl.ds(start, 2 * source_count), :] for index in range(dirs)], axis=1
        )
        out[row, 0] = both[:source_count]
        out[row, 1] = both[source_count:]
        return unused

    lax.fori_loop(0, dest_rows, row_step, 0, unroll=8)


def per_device(
    coarse_field,
    trans_table,
    partner_ids,
    partner_types,
    partner_count,
    child_count,
    child_octant,
    dir_angles,
    stencil_ids,
    stencil_weights,
):
    rows, _, source_count, kc_dev = coarse_field.shape
    slots = partner_ids.shape[1]
    type_count = trans_table.shape[0]
    fine_rows = child_octant.shape[0]
    ring_count = lax.axis_size("ring")
    dir_count = lax.axis_size("dir")
    zed = lax.axis_index("zed")
    ring = lax.axis_index("ring")
    dir_index = lax.axis_index("dir")
    fine_count = stencil_ids.shape[0] // 4
    kf_dev = fine_count // dir_count
    kc_pad = up(kc_dev, half * lanes)
    kf_pad = up(kf_dev, lanes)
    pad_dirs = kc_pad - kc_dev
    assert source_count == planes and kc_pad == half * lanes
    dest_rows = fine_rows // dir_count

    whole = pl.BlockSpec(memory_space=pltpu.VMEM)
    packed = pl.pallas_call(
        functools.partial(pack_kernel, source_count),
        out_shape=jax.ShapeDtypeStruct((source_count, rows * 2 * half, lanes), jnp.float32),
        in_specs=[whole],
        out_specs=whole,
        scratch_shapes=[pltpu.VMEM((half, rows * 2 * source_count, lanes), jnp.float32)],
        name="pack_sources",
    )(jnp.pad(coarse_field, ((0, 0), (0, 0), (0, 0), (0, pad_dirs))))
    arrived = lax.all_to_all(packed, "zed", split_axis=0, concat_axis=0, tiled=True)
    arrived = arrived.reshape(planes, rows, 2 * half, lanes)
    if ring_count == 2:
        edges = near_edge(arrived, ring)
        edge_rows = edges.shape[1]
        edges = lax.ppermute(edges, "ring", [(0, 1), (1, 0)])
        pieces = [
            arrived.reshape(planes * rows, 2 * half, lanes),
            edges.reshape(planes * edge_rows, 2 * half, lanes),
        ]
    else:
        pieces = [lax.all_gather(arrived, "ring", axis=1, tiled=True).reshape(-1, 2 * half, lanes)]

    plane_of = partner_ids // (ring_count * rows)
    ring_of = partner_ids // rows % ring_count
    local = partner_ids % rows
    live = jnp.arange(slots, dtype=jnp.int32)[None, :] < partner_count[:, None]
    if ring_count == 2:
        place = jnp.where(
            ring_of == ring,
            plane_of * rows + local,
            planes * rows + plane_of * edge_rows + edge_rank(local, rows),
        )
    else:
        place = partner_ids
    place = jnp.where(live, place, 0)
    kinds = jnp.where(live, partner_types, type_count)
    order = jnp.arange(rows, dtype=jnp.int32)
    bounds = jnp.sum(jnp.where(order[None, :] <= order[:, None], child_count[None, :], 0), axis=1)
    parent = jnp.sum(
        (bounds[None, :] <= jnp.arange(fine_rows, dtype=jnp.int32)[:, None]).astype(jnp.int32), axis=1
    )
    meta = jnp.concatenate([place.reshape(-1), kinds.reshape(-1), parent, child_octant])
    meta_stride = up(meta.shape[0], 8 * lanes)
    meta = jnp.pad(meta, (0, meta_stride - meta.shape[0])).reshape(1, meta_stride // lanes, lanes)
    meta = jnp.broadcast_to(meta, (planes,) + meta.shape[1:])
    meta = lax.all_to_all(meta, "zed", split_axis=0, concat_axis=0, tiled=True).reshape(-1)

    def blocks(table):
        return jnp.pad(table, ((0, 0), (0, pad_dirs))).reshape(-1, half, lanes)

    def doubled(table, sign):
        return jnp.concatenate([blocks(table), sign * blocks(table)], axis=1)

    table = jnp.pad(trans_table, ((0, 1), (0, 0), (0, pad_dirs))).reshape(-1, 2 * half, lanes)
    angles = lax.dynamic_slice_in_dim(dir_angles, dir_index * kc_dev, kc_dev, axis=1)
    octants = jnp.arange(8, dtype=jnp.int32)
    sign_x = 1.0 - 2.0 * (octants % 2).astype(jnp.float32)
    sign_y = 1.0 - 2.0 * (octants // 2 % 2).astype(jnp.float32)
    sign_z = 1.0 - 2.0 * (octants // 4).astype(jnp.float32)
    unit_x = jnp.sin(angles[0]) * jnp.cos(angles[1])
    unit_y = jnp.sin(angles[0]) * jnp.sin(angles[1])
    unit_z = jnp.cos(angles[0])
    phase = wave_scale * (
        sign_x[:, None] * unit_x[None, :] + sign_y[:, None] * unit_y[None, :] + sign_z[:, None] * unit_z[None, :]
    )
    cosine = doubled(jnp.cos(phase), 1.0)
    sine = doubled(jnp.sin(phase), -1.0)

    ids = lax.dynamic_slice_in_dim(stencil_ids, dir_index * kc_dev, kc_dev, axis=0).T
    weights = lax.dynamic_slice_in_dim(stencil_weights, dir_index * kc_dev, kc_dev, axis=0).T

    def interp(targets):
        matrix = jnp.zeros((targets.shape[0], kc_dev), jnp.float32)
        for point in range(ids.shape[0]):
            matrix = matrix + jnp.where(
                ids[point][None, :] == targets[:, None], weights[point][None, :], 0.0
            )
        return jnp.pad(matrix, ((0, 0), (0, pad_dirs)))

    first_fine = dir_index * kf_dev
    own = jnp.arange(kf_dev, dtype=jnp.int32)
    outside = jnp.concatenate(
        [jnp.arange(-rim, 0, dtype=jnp.int32), jnp.arange(kf_dev, kf_dev + rim, dtype=jnp.int32)]
    )
    matrix = jnp.pad(interp(first_fine + own).T, ((0, 0), (0, kf_pad - kf_dev)))
    spill = interp((first_fine + outside) % fine_count)
    blank = jnp.zeros_like(spill)
    spill_re = jnp.concatenate([spill, blank], axis=0)
    spill_im = jnp.concatenate([blank, spill], axis=0)

    field_rows = sum(piece.shape[0] for piece in pieces)
    message = (2 * dest_rows + 2 * half, kf_pad)
    local_fine = pl.pallas_call(
        functools.partial(fine_kernel, rows, slots, fine_rows, meta_stride, len(pieces)),
        out_shape=jax.ShapeDtypeStruct((planes, dir_count) + message, jnp.float32),
        in_specs=[pl.BlockSpec(memory_space=pltpu.SMEM)]
        + [pl.BlockSpec(memory_space=pl.ANY)] * len(pieces)
        + [whole] * 6,
        out_specs=whole,
        scratch_shapes=[
            pltpu.VMEM((field_rows, 2 * half, lanes), jnp.float32),
            pltpu.VMEM((field_rows, 2 * half, lanes), jnp.float32),
            pltpu.SemaphoreType.DMA((len(pieces),)),
            pltpu.VMEM((rows, 2 * half, lanes), jnp.float32),
            pltpu.VMEM((rows, 2 * half, lanes), jnp.float32),
            pltpu.VMEM((fine_rows * 2 * half, lanes), jnp.float32),
        ],
        compiler_params=pltpu.CompilerParams(vmem_limit_bytes=48 * 2**20),
        name="translate_and_interpolate",
    )(meta, *pieces, table, cosine, sine, matrix, spill_re, spill_im)

    parts = lax.all_to_all(
        local_fine.reshape((planes * dir_count,) + message),
        ("zed", "dir"),
        split_axis=0,
        concat_axis=0,
        tiled=True,
    )
    result = (dest_rows, 2, source_count, fine_count)
    if kf_dev == lanes and planes * dir_count * 2 * half == lanes and dest_rows <= lanes:
        return pl.pallas_call(
            functools.partial(join_kernel, source_count),
            out_shape=jax.ShapeDtypeStruct(result, jnp.float32),
            in_specs=[whole],
            out_specs=whole,
            scratch_shapes=[pltpu.VMEM((dir_count, dest_rows * 2 * source_count, lanes), jnp.float32)],
            name="join_parts",
        )(parts)
    parts = parts.reshape((planes, dir_count) + message)
    main = parts[:, :, : 2 * dest_rows, :kf_dev].reshape(planes, dir_count, 2, dest_rows, kf_dev)
    over = parts[:, :, 2 * dest_rows :, :dest_rows].reshape(planes, dir_count, 2, 2 * rim, dest_rows)
    low = jnp.roll(over[:, :, :, :rim], -1, axis=1)
    high = jnp.roll(over[:, :, :, rim:], 1, axis=1)
    middle = jnp.zeros((planes, dir_count, 2, kf_dev - 2 * rim, dest_rows), jnp.float32)
    fix = jnp.concatenate([high, middle, low], axis=3)
    total = main.transpose(3, 2, 0, 1, 4) + fix.transpose(4, 2, 0, 1, 3)
    return total.reshape(result)


def solution(mesh):
    boxes, dirs = mesh.shape["box"], mesh.shape["dir"]
    fine_mesh = Mesh(mesh.devices.reshape(planes, boxes // planes, dirs), ("zed", "ring", "dir"))
    box = ("zed", "ring")
    placed = (
        P(box, None, None, "dir"),
        P(None, None, "dir"),
        P(box, None),
        P(box, None),
        P(box),
        P(box),
        P(box),
        P(),
        P(),
        P(),
    )
    return jax.shard_map(
        per_device,
        mesh=fine_mesh,
        in_specs=placed,
        out_specs=P(("zed", "ring", "dir"), None, None, None),
        check_vma=False,
    )
```

time: 144 us -> 113 us (0.78)
  the two profiles are of different devices: /device:TPU:11 before, /device:TPU:0 now
where the time goes in v2:
time: 113 us
  Pallas kernels  35.2 us (31%)
  blocking collectives  34.2 us (30%)
  waiting for transfers between devices  24 us (21%)
  starting transfers between devices  11.3 us (10%)
  local copies, waits for them, and re-layouts  5.73 us (5%)
  other arithmetic  2.24 us (2%)
    all_to_all x1, blocking collectives, per_device(): lax.all_to_all(local_fine.reshape((planes * dir_count,) + message), ('zed...  34.2 us
    pallas_call x1, Pallas kernels, per_device(): pl.pallas_call(functools.partial(fine_kernel, rows, slots, fine_rows, met...  29.8 us
    all_to_all x1, waiting for transfers between devices, per_device(): lax.all_to_all(packed, 'zed', split_axis=0, concat_axis=0, tiled=True)  22.2 us
    all_to_all x1, starting transfers between devices, per_device(): lax.all_to_all(packed, 'zed', split_axis=0, concat_axis=0, tiled=True)  6.46 us
    all_to_all x1, starting transfers between devices, per_device(): lax.all_to_all(meta, 'zed', split_axis=0, concat_axis=0, tiled=True)  3.29 us
    pallas_call x1, Pallas kernels, per_device(): pl.pallas_call(functools.partial(join_kernel, source_count), out_shape=ja...  2.8 us
    pallas_call x1, Pallas kernels, per_device(): pl.pallas_call(functools.partial(pack_kernel, source_count), out_shape=ja...  2.58 us
    reshape x1, local copies, waits for them, and re-layouts, per_device(): jnp.pad(trans_table, ((0, 1), (0, 0), (0, pad_dirs)))  2.32 us
  transfers between devices with their start and end apart: 3, of which 3 were waited for; matrix products, arithmetic and copies ran while one was open for 6% of the time, Pallas kernels for 0%

profile of v2, /device:TPU:0, one launch (start us, length us, event | category | flops | bytes accessed | tf_op | source)
XLA Modules:
  0.0 113.0 jit_solution(16278427228525931861)
XLA Ops:
  0.0 2.6 %pack_sources.1 = f32[4,512,128]{2,1,0:T(8,128)} custom-call(f32[64,2,4,512]{3,2,1,0:T(4,128)} %field.1), custom_call_target="tpu_custom_call" | custom-call | tf_op jit(solution)/shard_map/pack_sources/pallas_call | solution.py:233
  2.6 6.5 %all-to-all-start.1 = ((f32[4,512,128]{2,1,0:T(8,128)}), f32[4,512,128]{2,1,0:T(8,128)S(1)}, u32[]{:S(2)}, u32[]{:S(2)}) async-start(f32[4,512,128]{2,1,0:T(8,128)} %pack_sources.1), calls=%async_computation.1 | async-start | bytes 2097152 | tf_op jit(solution)/shard_map/all_to_all | solution.py:241
  9.1 0.1 select_reduce_fusion
  9.3 0.1 fusion.8
  9.3 0.1 copy.14
  9.4 0.1 reshape.172
  9.6 0.1 copy.13
  9.7 0.1 reshape.171
  9.9 0.7 dynamic-slice_bitcast_fusion.1
  10.6 0.9 cosine_multiply_fusion
  11.6 0.1 convert_reduce_fusion
  11.8 0.2 fusion.24
  12.0 0.6 select_add_fusion.refs_5_
  12.6 22.2 %all-to-all-done.1 = f32[4,512,128]{2,1,0:T(8,128)S(1)} async-done(((f32[4,512,128]{2,1,0:T(8,128)}), f32[4,512,128]{2,1,0:T(8,128)S(1)}, u32[]{:S(2)}, u32[]{:S(2)}) %all-to-all-start.1) | async-done | bytes 1048608 | tf_op jit(solution)/shard_map/all_to_all | solution.py:241
  34.8 0.6 broadcast_in_dim.118
  35.4 3.3 %all-to-all-start = ((s32[4,40,128]{2,1,0:T(8,128)}), s32[4,40,128]{2,1,0:T(8,128)S(1)}, u32[]{:S(2)}, u32[]{:S(2)}) async-start(s32[4,40,128]{2,1,0:T(8,128)} %broadcast_in_dim.118), calls=%async_computation | async-start | bytes 163840 | tf_op jit(solution)/shard_map/all_to_all | solution.py:277
  38.8 1.6 %collective-permute-start = (f32[4,16,8,128]{3,2,1,0:T(8,128)S(1)}, f32[4,16,8,128]{3,2,1,0:T(8,128)S(1)}, u32[]{:S(2)}, u32[]{:S(2)}) collective-permute-start(f32[4,16,8,128]{3,2,1,0:T(8,128)S(1)} %bitcast.28), channel_id=1, source_target_pairs={{0,4},{4,0},{1,5},{5,1},{2,6},{6,2},{3,7},{7,3},{8,12},{12,8},{9,1... | collective-permute-start | bytes 786440 | tf_op jit(solution)/shard_map/ppermute | solution.py:246
  40.4 1.5 %pad.11 = f32[317,2,512]{2,1,0:T(2,128)} pad(f32[316,2,512]{2,1,0:T(2,128)S(1)} %copy-done.1, f32[]{:T(128)} %constant.234.clone.1), padding=0_1x0_0x0_0 | pad | bytes 2592772 | tf_op jit(solution)/shard_map/jit(_pad)/pad | solution.py:285
  41.9 2.3 %reshape.176.refs_2_ = f32[317,8,128]{2,1,0:T(8,128)S(1)} reshape(f32[317,2,512]{2,1,0:T(2,128)} %pad.11) | data formatting | bytes 2596864 | tf_op jit(solution)/shard_map/reshape | solution.py:285
  44.3 0.2 all-to-all-done
  44.5 1.6 %collective-permute-done = f32[4,16,8,128]{3,2,1,0:T(8,128)S(1)} collective-permute-done((f32[4,16,8,128]{3,2,1,0:T(8,128)S(1)}, f32[4,16,8,128]{3,2,1,0:T(8,128)S(1)}, u32[]{:S(2)}, u32[]{:S(2)}) %collective-permute-start) | collective-permute-done | bytes 262176 | tf_op jit(solution)/shard_map/ppermute | solution.py:246
  46.1 29.8 %translate_and_interpolate.1 = f32[4,4,136,128]{3,2,1,0:T(8,128)S(1)} custom-call(s32[20480]{0:T(1024)S(1)} %bitcast.26, f32[256,8,128]{2,1,0:T(8,128)S(1)} %bitcast.24, f32[64,8,128]{2,1,0:T(8,128)S(1)} %bitcast.27, f32[317,8,128]{2,1,0:T(8,128)S(1)} %reshape.176.refs_2_, f32[8,8,128]{2,1,0:T(8,128)S(1)} %pad_maximum_fusion.refs_3_, ...), custom_call_target="tpu_custom_call" | custom-call | tf_op jit(solution)/shard_map/translate_and_interpolate/pallas_call | solution.py:324
  75.9 34.2 %all_to_all.15.parts = f32[16,136,128]{2,1,0:T(8,128)} all-to-all(f32[16,136,128]{2,1,0:T(8,128)S(1)} %bitcast.25), channel_id=1, replica_groups=mesh['zed'=4,'ring'=2,'dir'=4] {'zed','dir'}, dimensions={0} | all-to-all | bytes 2228224 | tf_op jit(solution)/shard_map/all_to_all | solution.py:343
  110.2 2.8 %join_parts.1 = f32[64,2,4,512]{3,2,1,0:T(4,128)} custom-call(f32[16,136,128]{2,1,0:T(8,128)} %all_to_all.15.parts), custom_call_target="tpu_custom_call" | custom-call | tf_op jit(solution)/shard_map/join_parts/pallas_call | solution.py:352
  (29 shorter events, 0.3 us)
Async XLA Ops:
  0.0 9.8 %copy-start = (f32[2048,4]{0,1:T(4,128)S(1)}, f32[2048,4]{0,1:T(4,128)}, u32[]{:S(2)}) copy-start(f32[2048,4]{0,1:T(4,128)} %param.19) | copy-start | bytes 98308
  2.6 6.5 %copy-start.6 = (s32[64]{0:T(128)S(1)}, s32[64]{0:T(128)}, u32[]{:S(2)}) copy-start(s32[64]{0:T(128)} %param.15) | copy-start | bytes 772
  2.6 6.6 %copy-start.2 = (s32[64,30]{0,1:T(8,128)S(1)}, s32[64,30]{0,1:T(8,128)}, u32[]{:S(2)}) copy-start(s32[64,30]{0,1:T(8,128)} %param.12) | copy-start | bytes 23044
  2.6 6.6 %copy-start.3 = (s32[64,30]{0,1:T(8,128)S(1)}, s32[64,30]{0,1:T(8,128)}, u32[]{:S(2)}) copy-start(s32[64,30]{0,1:T(8,128)} %param.13) | copy-start | bytes 23044
  2.6 6.7 %copy-start.5 = (s32[64]{0:T(128)S(1)}, s32[64]{0:T(128)}, u32[]{:S(2)}) copy-start(s32[64]{0:T(128)} %param.14) | copy-start | bytes 772
  2.6 9.1 %copy-start.4 = (s32[256]{0:T(256)S(1)}, s32[256]{0:T(256)}, u32[]{:S(2)}) copy-start(s32[256]{0:T(256)} %param.16) | copy-start | bytes 3076
  2.6 32.2 %all-to-all-start.1 = ((f32[4,512,128]{2,1,0:T(8,128)}), f32[4,512,128]{2,1,0:T(8,128)S(1)}, u32[]{:S(2)}, u32[]{:S(2)}) async-start(f32[4,512,128]{2,1,0:T(8,128)} %pack_sources.1), calls=%async_computation.1 | async-start | bytes 2097152 | tf_op jit(solution)/shard_map/all_to_all | solution.py:241
  9.1 31.3 %copy-start.1 = (f32[316,2,512]{2,1,0:T(2,128)S(1)}, f32[316,2,512]{2,1,0:T(2,128)}, u32[]{:S(2)}) copy-start(f32[316,2,512]{2,1,0:T(2,128)} %param.11) | copy-start | bytes 3883012
  35.4 9.1 %all-to-all-start = ((s32[4,40,128]{2,1,0:T(8,128)}), s32[4,40,128]{2,1,0:T(8,128)S(1)}, u32[]{:S(2)}, u32[]{:S(2)}) async-start(s32[4,40,128]{2,1,0:T(8,128)} %broadcast_in_dim.118), calls=%async_computation | async-start | bytes 163840 | tf_op jit(solution)/shard_map/all_to_all | solution.py:277
  38.8 7.3 %collective-permute-start = (f32[4,16,8,128]{3,2,1,0:T(8,128)S(1)}, f32[4,16,8,128]{3,2,1,0:T(8,128)S(1)}, u32[]{:S(2)}, u32[]{:S(2)}) collective-permute-start(f32[4,16,8,128]{3,2,1,0:T(8,128)S(1)} %bitcast.28), channel_id=1, source_target_pairs={{0,4},{4,0},{1,5},{5,1},{2,6},{6,2},{3,7},{7,3},{8,12},{12,8},{9,1... | collective-permute-start | bytes 786440 | tf_op jit(solution)/shard_map/ppermute | solution.py:246
